TPU v7x, 128 devices: a whole 4x4x4 slice. The times are simulated.
128 devices in a mesh: dp: 16 (over z_lo, x, core), tensor: 8 (over y, z_hi).
Axes of the slice: x: 4, y: 4, z: 4 (z_hi: 2, z_lo: 2; z = z_hi * 2 + z_lo), core: 2. Of those that a mesh axis runs over, the one named last changes fastest.
Arguments:
- tokens: bfloat16 [1024, 8192], P('tensor', 'dp'), may hold values from -6 to 6
- segment_ids: int32 [1024], replicated, may hold values from 0 to 7, never falling along the last dimension, each value on 1 to 256 neighbouring positions
- gate_weight: bfloat16 [8192, 15360], P('dp', 'tensor'), may hold values from -0.0625 to 0.0625
- up_weight: bfloat16 [8192, 15360], P('dp', 'tensor'), may hold values from -0.0625 to 0.0625
- down_weight: bfloat16 [15360, 8192], P('tensor', 'dp'), may hold values from -0.046875 to 0.046875
- grad_out: bfloat16 [1024, 8192], P('tensor', 'dp'), may hold values from -6 to 6
Outputs:
- mixed: bfloat16 [1024, 8192], P('tensor', 'dp')
- grad_gate: float32 [8192, 15360], P('dp', 'tensor')
- grad_up: float32 [8192, 15360], P('dp', 'tensor')
- grad_down: float32 [15360, 8192], P('tensor', 'dp')
Inputs may be any that keep to these rules, and one draw needn't show every extreme that they name: `segment_ids`: document numbers never fall along the positions; each of the 8 documents has 1 to 256 positions and one has exactly 256.
All inputs are finite; a program needn't handle non-finite values.
Results may differ from a plain program's by a relative error of at most 0.005.
Values may be sent and summed in bfloat16 or wider, within the bound.
A program may use at most 192 MiB of HBM per device.

v0:
```python
import jax
import jax.numpy as jnp
from jax import lax
from jax.sharding import PartitionSpec as P

NSEG = 8


def contract_rows(left, right):
    return lax.dot_general(
        left, right, (((0,), (0,)), ((), ())), preferred_element_type=jnp.float32
    )


def gate_grads(dhidden, gate, up):
    sig = jax.nn.sigmoid(gate)
    dgate = (dhidden * up * sig * (1.0 + gate * (1.0 - sig))).astype(jnp.bfloat16)
    dup = (dhidden * gate * sig).astype(jnp.bfloat16)
    return (dgate, dup)


def shards(tokens, segment_ids, gate_weight, up_weight, down_weight, grad_out):
    rows_local = tokens.shape[0]
    onehot = (segment_ids[:, None] == jnp.arange(NSEG, dtype=jnp.int32)[None, :]).astype(
        jnp.float32
    )
    lengths = jnp.sum(onehot, axis=0)
    row_weight = lax.rsqrt(jnp.sum(onehot * lengths[None, :], axis=1))
    gathered = lax.all_gather(tokens, "tensor", axis=0, tiled=True)
    block = gathered
    gate_part = jnp.dot(block, gate_weight, preferred_element_type=jnp.float32)
    up_part = jnp.dot(block, up_weight, preferred_element_type=jnp.float32)
    summed = lax.psum(jnp.stack((gate_part, up_part), axis=1), "dp")
    gate = summed[:, 0]
    up = summed[:, 1]
    hidden = (gate * jax.nn.sigmoid(gate) * up).astype(jnp.bfloat16)
    block = hidden
    mixed = lax.psum_scatter(
        jnp.dot(block, down_weight, preferred_element_type=jnp.float32),
        "tensor",
        scatter_dimension=0,
        tiled=True,
    ).astype(jnp.bfloat16)
    own_weight = lax.dynamic_slice_in_dim(
        row_weight, lax.axis_index("tensor") * rows_local, rows_local, 0
    )
    scaled_local = (grad_out.astype(jnp.float32) * own_weight[:, None]).astype(jnp.bfloat16)
    scaled = lax.all_gather(scaled_local, "tensor", axis=0, tiled=True)
    grad_down = contract_rows(hidden, scaled)
    block = scaled
    dhidden = lax.psum(
        lax.dot_general(
            block, down_weight, (((1,), (1,)), ((), ())), preferred_element_type=jnp.float32
        ),
        "dp",
    )
    dgate, dup = gate_grads(dhidden, gate, up)
    grad_gate = contract_rows(gathered, dgate)
    grad_up = contract_rows(gathered, dup)
    return (mixed, grad_gate, grad_up, grad_down)


def solution(mesh):
    placed = (
        P("tensor", "dp"),
        P(),
        P("dp", "tensor"),
        P("dp", "tensor"),
        P("tensor", "dp"),
        P("tensor", "dp"),
    )
    return jax.shard_map(
        shards,
        mesh=mesh,
        in_specs=placed,
        out_specs=(P("tensor", "dp"), P("dp", "tensor"), P("dp", "tensor"), P("tensor", "dp")),
        check_vma=False,
    )
```

profile of v0, /device:TPU:8, one launch (start us, length us, event | category | flops | bytes accessed | tf_op | source)
XLA Modules:
  0.0 474.2 jit_solution(7616373254661690000)
XLA Ops:
  7.2 0.0 copy-start
  7.2 0.0 all-gather.3.cloned.1.call-start
  7.2 0.7 all-gather.3.cloned.1.call-update
  7.9 0.0 all-gather.5.cloned.1.call-start
  8.0 0.8 convert_reduce_fusion
  8.8 0.8 select_reduce_fusion
  9.6 0.1 dynamic_slice.3
  9.6 1.6 multiply_convert_fusion.9
  11.3 0.0 all-gather.5.cloned.1.call-update
  11.3 0.0 all-reduce.3.cloned.1.call-start
  11.4 48.5 %all-gather.3.cloned.1.call-done = bf16[1024,512]{1,0:T(8,128)(2,1)} async-done(((bf16[128,512]{1,0:T(8,128)(2,1)}), bf16[1024,512]{1,0:T(8,128)(2,1)}) %all-gather.3.cloned.1.call-update) | async-done | bytes 1048592 | tf_op jit(solution)/shard_map/all_gather | solution.py:29
  59.9 7.4 %convolution_bitcast_fusion = f32[1024,1,1920]{2,0,1:T(8,128)} fusion(bf16[1024,512]{1,0:T(8,128)(2,1)} %all-gather.3.cloned.1.call-done, bf16[512,1920]{1,0:T(8,128)(2,1)} %param.9), kind=kOutput, calls=%fused_computation.7 | convolution fusion | flops 2013265920 | bytes 10878976 | tf_op jit(solution)/shard_map/dot_general | solution.py:32
  67.3 0.0 copy-done.3
  67.3 5.5 %convolution_bitcast_fusion.1 = f32[1024,1,1920]{2,0,1:T(8,128)} fusion(bf16[1024,512]{1,0:T(8,128)(2,1)S(1)} %copy-done.4, bf16[512,1920]{1,0:T(8,128)(2,1)S(1)} %copy-done.3), kind=kOutput, calls=%fused_computation.8 | convolution fusion | flops 2013265920 | bytes 10878976 | tf_op jit(solution)/shard_map/dot_general | solution.py:31
  72.8 12.0 %pad_maximum_fusion = f32[1024,2,1920]{2,0,1:T(8,128)} fusion(f32[1024,1,1920]{2,0,1:T(8,128)} %convolution_bitcast_fusion, f32[1024,1,1920]{2,0,1:T(8,128)} %convolution_bitcast_fusion.1), kind=kLoop, calls=%fused_computation | loop fusion | flops 3932160 | bytes 31457280 | tf_op jit(solution)/shard_map/stack | solution.py:33
  84.8 24.1 %all-gather.5.cloned.1.call-done = bf16[1024,512]{1,0:T(8,128)(2,1)} async-done(((bf16[128,512]{1,0:T(8,128)(2,1)}), bf16[1024,512]{1,0:T(8,128)(2,1)}) %all-gather.5.cloned.1.call-update) | async-done | bytes 1048592 | tf_op jit(solution)/shard_map/all_gather | solution.py:48
  108.9 6.7 %fusion.7 = f32[1024,1920]{1,0:T(8,128)} fusion(bf16[1024,512]{1,0:T(8,128)(2,1)} %all-gather.5.cloned.1.call-done, bf16[1920,512]{1,0:T(8,128)(2,1)S(1)} %copy-done), kind=kOutput, calls=%fused_computation.20 | convolution fusion | flops 2013265920 | bytes 10878976 | tf_op jit(solution)/shard_map/dot_general | solution.py:52
  115.6 0.0 all-reduce.3.cloned.1.call-update
  115.6 0.2 reduce-scatter.2.cloned.1.call-start
  115.9 263.6 %all-reduce.3.cloned.1.call-done = (f32[1024,2,1920]{2,0,1:T(8,128)}, f32[1024,1920]{1,0:T(8,128)}) async-done(((f32[1024,2,1920]{2,0,1:T(8,128)}, f32[1024,1920]{1,0:T(8,128)}), (f32[1024,2,1920]{2,0,1:T(8,128)}, f32[1024,1920]{1,0:T(8,128)})) %all-reduce.3.cloned.1.call-update) | async-done | bytes 23592976 | tf_op jit(solution)/shard_map/psum | solution.py:33
  379.4 6.7 %multiply_convert_fusion.2 = bf16[1024,1920]{1,0:T(8,128)(2,1)S(1)} fusion(f32[1024,2,1920]{2,0,1:T(8,128)} %get-tuple-element.12), kind=kLoop, calls=%fused_computation.5 | loop fusion | flops 11796480 | bytes 19660800 | tf_op jit(solution)/shard_map/convert_element_type | solution.py:36
  386.1 1.9 copy-done.2
  388.0 3.7 fusion.6
  391.7 0.0 reduce-scatter.2.cloned.1.call-update
  391.7 12.1 %fusion.2 = f32[512,1920]{0,1:T(8,128)} fusion(bf16[1024,512]{1,0:T(8,128)(2,1)S(1)} %copy-done.4, f32[1024,1920]{1,0:T(8,128)} %get-tuple-element.13, f32[1024,2,1920]{2,0,1:T(8,128)} %get-tuple-element.12), kind=kOutput, calls=%fused_computation.11 | convolution fusion | flops 2032926720 | bytes 28573696 | tf_op jit(solution)/shard_map/dot_general | solution.py:10
  403.8 5.5 %copy.12 = f32[512,1920]{1,0:T(8,128)} copy(f32[512,1920]{0,1:T(8,128)} %fusion.2) | data formatting | bytes 7864320
  409.3 10.1 %fusion.3 = f32[512,1920]{0,1:T(8,128)} fusion(bf16[1024,512]{1,0:T(8,128)(2,1)S(1)} %copy-done.4, f32[1024,1920]{1,0:T(8,128)} %get-tuple-element.13, f32[1024,2,1920]{2,0,1:T(8,128)} %get-tuple-element.12), kind=kOutput, calls=%fused_computation.12 | convolution fusion | flops 2025062400 | bytes 20709376 | tf_op jit(solution)/shard_map/dot_general | solution.py:10
  419.4 5.6 %copy.13 = f32[512,1920]{1,0:T(8,128)} copy(f32[512,1920]{0,1:T(8,128)} %fusion.3) | data formatting | bytes 7864320
  425.0 0.0 copy-done.5
  425.0 6.3 %fusion.8 = f32[1920,512]{1,0:T(8,128)} fusion(bf16[1024,1920]{1,0:T(8,128)(2,1)} %copy-done.2, bf16[1024,512]{1,0:T(8,128)(2,1)S(1)} %copy-done.5), kind=kOutput, calls=%fused_computation.21 | convolution fusion | flops 2013265920 | bytes 8912896 | tf_op jit(solution)/shard_map/dot_general | solution.py:10
  431.3 34.7 %reduce-scatter.2.cloned.1.call-done = f32[128,512]{1,0:T(8,128)} async-done(((f32[1024,512]{1,0:T(8,128)}), f32[128,512]{1,0:T(8,128)}) %reduce-scatter.2.cloned.1.call-update) | async-done | bytes 262160 | tf_op jit(solution)/shard_map/reduce_scatter | solution.py:38
  466.0 1.6 convert_element_type.22
  (9 shorter events, 0.0 us)
Async XLA Ops:
  7.2 101.7 %copy-start = (bf16[1920,512]{1,0:T(8,128)(2,1)S(1)}, bf16[1920,512]{1,0:T(8,128)(2,1)}, u32[]{:S(2)}) copy-start(bf16[1920,512]{1,0:T(8,128)(2,1)} %param.10) | copy-start | bytes 5898244
  7.2 52.7 %all-gather.3.cloned.1.call-start = ((), (), s32[]{:S(2)}) async-start(), calls=%async_computation.1 | async-start | bytes 1179648 | tf_op jit(solution)/shard_map/all_gather | solution.py:29
  7.9 101.0 %all-gather.5.cloned.1.call-start = ((), (), s32[]{:S(2)}) async-start(), calls=%async_computation.3 | async-start | bytes 1179648 | tf_op jit(solution)/shard_map/all_gather | solution.py:48
  11.3 368.1 %all-reduce.3.cloned.1.call-start = ((), (), s32[]{:S(2)}) async-start(), calls=%async_computation.4 | async-start | bytes 47185920 | tf_op jit(solution)/shard_map/psum | solution.py:33
  59.9 7.4 %copy-start.3 = (bf16[512,1920]{1,0:T(8,128)(2,1)S(1)}, bf16[512,1920]{1,0:T(8,128)(2,1)}, u32[]{:S(2)}) copy-start(bf16[512,1920]{1,0:T(8,128)(2,1)} %param.8) | copy-start | bytes 5898244
  59.9 7.4 %copy-start.4 = (bf16[1024,512]{1,0:T(8,128)(2,1)S(1)}, bf16[1024,512]{1,0:T(8,128)(2,1)}, u32[]{:S(2)}) copy-start(bf16[1024,512]{1,0:T(8,128)(2,1)} %all-gather.3.cloned.1.call-done) | copy-start | bytes 3145732
  115.6 350.4 %reduce-scatter.2.cloned.1.call-start = ((), (), s32[]{:S(2)}) async-start(), calls=%async_computation.2 | async-start | bytes 2359296 | tf_op jit(solution)/shard_map/reduce_scatter | solution.py:38
  386.1 1.9 copy-start.2
  419.4 5.6 %copy-start.5 = (bf16[1024,512]{1,0:T(8,128)(2,1)S(1)}, bf16[1024,512]{1,0:T(8,128)(2,1)}, u32[]{:S(2)}) copy-start(bf16[1024,512]{1,0:T(8,128)(2,1)} %all-gather.5.cloned.1.call-done) | copy-start | bytes 3145732
  419.4 48.3 %copy-start.1 = (bf16[1920,512]{1,0:T(8,128)(2,1)S(1)}, bf16[1920,512]{1,0:T(8,128)(2,1)}, u32[]{:S(2)}) copy-start(bf16[1920,512]{1,0:T(8,128)(2,1)} %param.10) | copy-start | bytes 5898244
Sparse Core Ops, SparseCore 0:
  10.4 49.4 all-gather.2
  62.8 46.0 all-gather.4
  115.7 263.6 all-reduce.2
  391.9 74.1 reduce-scatter.1
where the time goes:
time: 475 us; the launch traced here: 474 us
  waiting for transfers between devices  372 us (78%)
  matrix products  51.8 us (11%)
  other arithmetic  23.5 us (5%)
  between operations  13.8 us (3%)
  local copies, waits for them, and re-layouts  13.1 us (3%)
    psum x1, waiting for transfers between devices, shards(): summed = lax.psum(jnp.stack((gate_part, up_part), axis=1), 'dp')  264 us
    all_gather x1, waiting for transfers between devices, shards(): gathered = lax.all_gather(tokens, 'tensor', axis=0, tiled=True)  48.5 us
    reduce_scatter x1, waiting for transfers between devices, shards(): lax.psum_scatter(jnp.dot(block, down_weight, preferred_element_type=jnp.f...  34.7 us
    dot_general x3, matrix products, contract_rows(): lax.dot_general(left, right, (((0,), (0,)), ((), ())), preferred_element_...  28.5 us
    all_gather x1, waiting for transfers between devices, shards(): scaled = lax.all_gather(scaled_local, 'tensor', axis=0, tiled=True)  24.1 us
    unnamed x14, local copies, waits for them, and re-layouts  13 us
    another operation x1, other arithmetic, shards(): summed = lax.psum(jnp.stack((gate_part, up_part), axis=1), 'dp')  12 us
  transfers between devices with their start and end apart: 4, of which 4 were waited for; matrix products, arithmetic and copies ran while one was open for 14% of the time, Pallas kernels for 0%

commit v1 on v0

v1 whole, which is shorter than its diff:
```python
import jax
import jax.numpy as jnp
from jax import lax
from jax.experimental import pallas as pl
from jax.experimental.pallas import tpu as pltpu
from jax.sharding import PartitionSpec as P

NSEG = 8
SLOTS = 8
ROWS = 128
HALF = 64
SEG = 16
WIDTH = 512
UNITS = 1920
TILE = 128
MESH = pl.DeviceIdType.MESH
BF16 = jnp.bfloat16
F32 = jnp.float32
DOT_COLUMNS = ((0, 512), (512, 512), (1024, 512), (1536, 384))

CA = 1152
CB = UNITS - CA
OA = -(-CA // (2 * TILE)) * TILE
KA = CA - OA
OB = -(-CB // (2 * TILE)) * TILE
KB = CB - OB
OL = OB // (2 * TILE) * TILE
OR = OB - OL

NAMES = (
    "core0", "core1", "core2", "x1p", "x1m", "x2p", "x2m", "zred", "zgat", "g1p", "g1m", "g2p", "g2m", "cgat",
    "mix", "y0", "y1p", "y1m", "y2p", "y2m", "k1p", "k1m", "k2p", "k2m", "k3",
)
KIND = {name: i for i, name in enumerate(NAMES)}


def exchange_kernel(
    ids_hbm, tokens_hbm, grad_out_hbm, wg_hbm, wu_hbm, wd_hbm,
    mown, gat, tokt, hidt, hh,
    ids, grad_out, wg, wu, wd, acc, cs, cr, x1s, x1a, x1b, x2s, x2r, zs, zr,
    y0s, y0r, y1s, y1a, y1b, y2s, y2r, ms, mr,
    ss, rs, ts, tr, ws, own_sems,
):
    inputs = [
        pltpu.make_async_copy(a, b, own_sems.at[k])
        for k, (a, b) in enumerate(
            ((ids_hbm, ids), (grad_out_hbm, grad_out), (tokens_hbm, gat.at[0, :, :WIDTH]))
        )
    ]
    for copy in inputs:
        copy.start()
    weights = [
        pltpu.make_async_copy(a, b, ws.at[k])
        for k, (a, b) in enumerate(((wg_hbm, wg), (wu_hbm, wu), (wd_hbm, wd)))
    ]
    for copy in weights:
        copy.start()

    dp = lax.axis_index("dp")
    tn = lax.axis_index("tensor")
    w, x, q = dp // 8, (dp // 2) % 4, dp % 2
    y, h = tn // 2, tn % 2
    xp, xm, xo = (x + 1) % 4, (x + 3) % 4, (x + 2) % 4

    def dpdev(w=w, x=x, q=q):
        return (w * 8 + x * 2 + q, tn)

    def tdev(dy, dh):
        return (dp, ((y + dy) % 4) * 2 + (h + dh) % 2)

    core, right, left, zmate = dpdev(q=1 - q), dpdev(x=xp), dpdev(x=xm), dpdev(w=1 - w)
    offsets = [(0, 0), (1, 0), (3, 0), (0, 1), (1, 1), (3, 1), (2, 1), (2, 0)]

    barrier = pltpu.get_barrier_semaphore()
    partners = [core, right, left, zmate] + [tdev(*o) for o in offsets[1:]]
    for p in partners:
        pl.semaphore_signal(barrier, inc=1, device_id=p, device_id_type=MESH)

    for copy in inputs:
        copy.wait()
    all_ids = ids[...]
    own_ids = ids[pl.ds(tn, 1), :]
    row = jnp.zeros((1, ROWS), F32)
    for s in range(NSEG):
        length = jnp.sum(jnp.where(all_ids == s, 1.0, 0.0), axis=(0, 1), keepdims=True)
        row = jnp.where(own_ids == s, lax.rsqrt(length), row)
    square = jnp.broadcast_to(row, (ROWS, ROWS))
    on_diagonal = lax.broadcasted_iota(jnp.int32, (ROWS, ROWS), 0) == lax.broadcasted_iota(
        jnp.int32, (ROWS, ROWS), 1
    )
    column = jnp.sum(jnp.where(on_diagonal, square, 0.0), axis=1, keepdims=True)
    gat[0, :, WIDTH:] = (grad_out[...].astype(F32) * column).astype(BF16)

    pl.semaphore_wait(barrier, len(partners))

    def rows_of(xx):
        return pl.ds(pl.multiple_of(q * HALF + xx * SEG, SEG), SEG)

    def seg_of(xx):
        return pl.ds(pl.multiple_of(xx * SEG, SEG), SEG)

    def half_of(qq):
        return pl.ds(pl.multiple_of(qq * HALF, HALF), HALF)

    def cols_of(start, size):
        return pl.ds(pl.multiple_of(start, TILE), size)

    def msg(name, c, src, dst, dev):
        kind = KIND[name]
        return pltpu.make_async_remote_copy(
            src_ref=src, dst_ref=dst, send_sem=ss.at[kind, c], recv_sem=rs.at[kind, c],
            device_id=dev, device_id_type=MESH,
        )

    def tok_msg(slot, src, dev):
        return pltpu.make_async_remote_copy(
            src_ref=src, dst_ref=gat.at[slot], send_sem=ts.at[slot], recv_sem=tr.at[slot],
            device_id=dev, device_id_type=MESH,
        )

    def in_place(name, c, rows, cols, dev):
        ref = hh.at[c, :, rows, cols]
        return msg(name, c, ref, ref, dev)

    own_a, mate_a = cols_of(w * KA, OA), cols_of((1 - w) * KA, OA)
    out_a, in_a = cols_of(w * OA, KA), cols_of((1 - w) * OA, KA)
    own_b, mate_b = cols_of(CA + w * KB, OB), cols_of(CA + (1 - w) * KB, OB)
    own_b_left = cols_of(CA + w * KB, OL)
    own_b_right = cols_of(CA + w * KB + OL, OR)
    out_b, in_b = cols_of(CA + w * OB, KB), cols_of(CA + (1 - w) * OB, KB)
    all_a, lo_a, hi_a = pl.ds(0, CA), pl.ds(0, OA), pl.ds(OA, KA)

    def m_core(c, k):
        return msg(f"core{k}", c, cs.at[c % 2, k], cr.at[c % 3, k], core)

    def m_x1p(c):
        return msg("x1p", c, x1s.at[c, :, :, lo_a], x1a.at[c], right)

    def m_x1m(c):
        return msg("x1m", c, x1s.at[c, :, :, hi_a], x1b.at[c], left)

    def m_x2p(c):
        return msg("x2p", c, x2s.at[c, 0], x2r.at[c, 0], right)

    def m_x2m(c):
        return msg("x2m", c, x2s.at[c, 1], x2r.at[c, 1], left)

    def m_zred(c):
        return msg("zred", c, zs.at[c], zr.at[c], zmate)

    def m_zgat(c, cols):
        return in_place("zgat", c, rows_of(x), cols, zmate)

    def m_g1p(c, xx):
        return in_place("g1p", c, rows_of(xx), all_a, right)

    def m_g1m(c, xx):
        return in_place("g1m", c, rows_of(xx), all_a, left)

    def m_g2p(c, xx):
        return in_place("g2p", c, rows_of(xx), hi_a, right)

    def m_g2m(c, xx):
        return in_place("g2m", c, rows_of(xx), lo_a, left)

    def m_y0(c):
        return msg("y0", c, y0s.at[c], y0r.at[c], zmate)

    def m_y1p(c):
        return msg("y1p", c, y1s.at[c, :, :, :OL], y1a.at[c], right)

    def m_y1m(c):
        return msg("y1m", c, y1s.at[c, :, :, OL:], y1b.at[c], left)

    def m_y2p(c):
        return msg("y2p", c, y2s.at[c, 0], y2r.at[c, 0], right)

    def m_y2m(c):
        return msg("y2m", c, y2s.at[c, 1], y2r.at[c, 1], left)

    def m_k1p(c, xx):
        return in_place("k1p", c, rows_of(xx), own_b, right)

    def m_k1m(c, xx):
        return in_place("k1m", c, rows_of(xx), own_b, left)

    def m_k2p(c, xx):
        return in_place("k2p", c, rows_of(xx), own_b_right, right)

    def m_k2m(c, xx):
        return in_place("k2m", c, rows_of(xx), own_b_left, left)

    def m_k3(c, cols):
        return in_place("k3", c, half_of(q), cols, zmate)

    def m_cgat(c, qq):
        ref = hh.at[c, :, half_of(qq), :]
        return msg("cgat", c, ref, ref, core)

    def m_mix(c):
        dy = jnp.where(c >= 6, 2, c % 3 + c % 3 // 2)
        return msg("mix", c, ms.at[c], mr.at[c], tdev(dy, (c + 1) // 4 % 2))

    for s in (1, 2, 3, 7):
        dy, dh = offsets[s]
        tok_msg(s, gat.at[0], tdev(-dy % 4, dh)).start()
    for copy in weights:
        copy.wait()

    def a_partials(c):
        @pl.when((c != 0) & (c != 3))
        def _():
            tok_msg(c, gat.at[0], core).wait_recv()

        both = jnp.concatenate([gat[c, half_of(1 - q), :], gat[c, half_of(q), :]], axis=0)
        tok, sc = both[:, :WIDTH], both[:, WIDTH:]
        for k, mat in enumerate((wg, wu, wd)):
            for n0, nw in DOT_COLUMNS:
                cols = slice(n0, n0 + nw)
                if k < 2:
                    part = jnp.dot(tok, mat[:, cols], preferred_element_type=F32)
                else:
                    part = lax.dot_general(
                        sc, mat[cols, :], (((1,), (1,)), ((), ())), preferred_element_type=F32
                    )
                cs[c % 2, k, :, cols] = part[:HALF]
                acc[c % 5, k, :, cols] = part[HALF:]
            m_core(c, k).start()

    def forward_tokens():
        tok_msg(3, gat.at[0], core).wait_recv()
        for s in (4, 5, 6):
            tok_msg(s, gat.at[3], tdev(-offsets[s][0] % 4, 0)).start()

    def b_stage(c):
        a = c % 5
        for k in range(3):
            m_core(c, k).wait_recv()
        acc[a] += cr[c % 3]
        x1s[c] = acc[a, :, seg_of(xo), :CA].astype(BF16)
        m_x1p(c).start()
        m_x1m(c).start()
        y0s[c] = acc[a, :, :, mate_b].astype(BF16)
        m_y0(c).start()
        for k in range(3):
            m_core(c, k).wait_send()

    def c_stage(c):
        a = c % 5
        m_x1p(c).wait_recv()
        m_x1m(c).wait_recv()
        acc[a, :, seg_of(xp), :OA] += x1a[c].astype(F32)
        acc[a, :, seg_of(xm), OA:CA] += x1b[c].astype(F32)
        x2s[c, 0] = acc[a, :, seg_of(xp), :CA].astype(BF16)
        x2s[c, 1] = acc[a, :, seg_of(xm), :CA].astype(BF16)
        m_x2p(c).start()
        m_x2m(c).start()

    def c2_stage(c):
        a = c % 5
        m_y0(c).wait_recv()
        acc[a, :, :, own_b] += y0r[c].astype(F32)
        y1s[c] = acc[a, :, seg_of(xo), own_b].astype(BF16)
        m_y1p(c).start()
        m_y1m(c).start()

    def d_stage(c):
        a = c % 5
        m_x2p(c).wait_recv()
        m_x2m(c).wait_recv()
        acc[a, :, seg_of(x), :CA] += x2r[c, 0].astype(F32) + x2r[c, 1].astype(F32)
        zs[c] = acc[a, :, seg_of(x), mate_a].astype(BF16)
        m_zred(c).start()

    def d2_stage(c):
        a = c % 5
        m_y1p(c).wait_recv()
        m_y1m(c).wait_recv()
        acc[a, :, seg_of(xp), own_b_left] += y1a[c].astype(F32)
        acc[a, :, seg_of(xm), own_b_right] += y1b[c].astype(F32)
        y2s[c, 0] = acc[a, :, seg_of(xp), own_b].astype(BF16)
        y2s[c, 1] = acc[a, :, seg_of(xm), own_b].astype(BF16)
        m_y2p(c).start()
        m_y2m(c).start()

    def finish_units(c, tot, cols):
        gate, up, dhid = tot[0], tot[1], tot[2]
        sig = jax.nn.sigmoid(gate)
        hh[c, 0, rows_of(x), cols] = (gate * sig * up).astype(BF16)
        hh[c, 1, rows_of(x), cols] = (dhid * up * sig * (1.0 + gate * (1.0 - sig))).astype(BF16)
        hh[c, 2, rows_of(x), cols] = (dhid * gate * sig).astype(BF16)

    def e_stage(c):
        a = c % 5
        m_zred(c).wait_recv()
        finish_units(c, acc[a, :, seg_of(x), own_a] + zr[c].astype(F32), own_a)
        m_zgat(c, out_a).start()

    def e2_stage(c):
        a = c % 5
        m_y2p(c).wait_recv()
        m_y2m(c).wait_recv()
        tot = acc[a, :, seg_of(x), own_b] + y2r[c, 0].astype(F32) + y2r[c, 1].astype(F32)
        finish_units(c, tot, own_b)
        m_k1p(c, x).start()
        m_k1m(c, x).start()

    def f_stage(c):
        m_zgat(c, in_a).wait_recv()
        m_g1p(c, x).start()
        m_g1m(c, x).start()

    def f2_stage(c):
        m_k1p(c, xm).wait_recv()
        m_k2p(c, xm).start()
        m_k1m(c, xp).wait_recv()
        m_k2m(c, xp).start()

    def g_stage(c):
        m_g1p(c, xm).wait_recv()
        m_g2p(c, xm).start()
        m_g1m(c, xp).wait_recv()
        m_g2m(c, xp).start()

    def g2_stage(c):
        m_k2p(c, xo).wait_recv()
        m_k2m(c, xo).wait_recv()
        m_k3(c, out_b).start()

    def h_stage(c):
        m_g2p(c, xo).wait_recv()
        m_g2m(c, xo).wait_recv()
        m_k3(c, in_b).wait_recv()
        m_cgat(c, q).start()

    def i_stage(c):
        m_cgat(c, 1 - q).wait_recv()
        part = jnp.dot(hh[c, 0], wd[...], preferred_element_type=F32)

        @pl.when(c == 0)
        def _():
            mown[...] = part

        @pl.when(c != 0)
        def _():
            ms[c] = part.astype(BF16)
            m_mix(c).start()

        tokens_c = cols_of(c * ROWS, ROWS)
        hidt[:, tokens_c] = hh[c, 0].T
        tokt[:, tokens_c] = gat[c, :, :WIDTH].T

    plan = [
        (e_stage, 5, False), (c_stage, 2, False), (g2_stage, 8, True), (g_stage, 11, True),
        (f_stage, 9, True), (b_stage, 1, False), (d_stage, 3, False), (f2_stage, 6, True),
        (a_partials, 0, False), (h_stage, 12, True), (e2_stage, 4, False), (c2_stage, 2, False),
        (d2_stage, 3, False), (i_stage, 13, True),
    ]
    last = max(lag for _, lag, _ in plan)

    def step(i, carry):
        for stage, lag, back in plan:
            j = i - lag
            c = (j + 1) % SLOTS if back else j

            @pl.when((j >= 0) & (j < SLOTS))
            def _(stage=stage, c=c):
                stage(c)

        @pl.when(i == 2)
        def _():
            forward_tokens()

        return carry

    lax.fori_loop(0, SLOTS + last, step, 0)

    def finish(c, carry):
        m_mix(c).wait_recv()
        mown[...] += mr[c].astype(F32)
        return carry

    lax.fori_loop(1, SLOTS, finish, 0)

    def drain(c, carry):
        for message in (
            m_x1p(c), m_x1m(c), m_x2p(c), m_x2m(c), m_zred(c), m_zgat(c, out_a),
            m_g1p(c, x), m_g1m(c, x), m_g2p(c, xm), m_g2m(c, xp), m_cgat(c, q),
            m_y0(c), m_y1p(c), m_y1m(c), m_y2p(c), m_y2m(c), m_k1p(c, x), m_k1m(c, x),
            m_k2p(c, xm), m_k2m(c, xp), m_k3(c, out_b),
        ):
            message.wait_send()

        @pl.when(c != 0)
        def _():
            m_mix(c).wait_send()
            tok_msg(c, gat.at[0], core).wait_send()

        return carry

    lax.fori_loop(0, SLOTS, drain, 0)


def exchange(ids, tokens, grad_out, wg, wu, wd):
    vmem = pl.BlockSpec(memory_space=pltpu.VMEM)
    hbm = pl.BlockSpec(memory_space=pltpu.HBM)
    total = SLOTS * ROWS
    kinds = len(NAMES)
    return pl.pallas_call(
        exchange_kernel,
        name="exchange",
        out_shape=(
            pltpu.VMEM((ROWS, WIDTH), F32),
            pltpu.VMEM((SLOTS, ROWS, 2 * WIDTH), BF16),
            pltpu.VMEM((WIDTH, total), BF16),
            pltpu.VMEM((UNITS, total), BF16),
            pltpu.VMEM((SLOTS, 3, ROWS, UNITS), BF16),
        ),
        in_specs=[hbm] * 6,
        out_specs=(vmem,) * 5,
        scratch_shapes=[
            pltpu.VMEM((SLOTS, ROWS), jnp.int32),
            pltpu.VMEM((ROWS, WIDTH), BF16),
            pltpu.VMEM((WIDTH, UNITS), BF16),
            pltpu.VMEM((WIDTH, UNITS), BF16),
            pltpu.VMEM((UNITS, WIDTH), BF16),
            pltpu.VMEM((5, 3, HALF, UNITS), F32),
            pltpu.VMEM((2, 3, HALF, UNITS), F32),
            pltpu.VMEM((3, 3, HALF, UNITS), F32),
            pltpu.VMEM((SLOTS, 3, SEG, CA), BF16),
            pltpu.VMEM((SLOTS, 3, SEG, OA), BF16),
            pltpu.VMEM((SLOTS, 3, SEG, KA), BF16),
            pltpu.VMEM((SLOTS, 2, 3, SEG, CA), BF16),
            pltpu.VMEM((SLOTS, 2, 3, SEG, CA), BF16),
            pltpu.VMEM((SLOTS, 3, SEG, OA), BF16),
            pltpu.VMEM((SLOTS, 3, SEG, OA), BF16),
            pltpu.VMEM((SLOTS, 3, HALF, OB), BF16),
            pltpu.VMEM((SLOTS, 3, HALF, OB), BF16),
            pltpu.VMEM((SLOTS, 3, SEG, OB), BF16),
            pltpu.VMEM((SLOTS, 3, SEG, OL), BF16),
            pltpu.VMEM((SLOTS, 3, SEG, OR), BF16),
            pltpu.VMEM((SLOTS, 2, 3, SEG, OB), BF16),
            pltpu.VMEM((SLOTS, 2, 3, SEG, OB), BF16),
            pltpu.VMEM((SLOTS, ROWS, WIDTH), BF16),
            pltpu.VMEM((SLOTS, ROWS, WIDTH), BF16),
            pltpu.SemaphoreType.DMA((kinds, SLOTS)),
            pltpu.SemaphoreType.DMA((kinds, SLOTS)),
            pltpu.SemaphoreType.DMA((SLOTS,)),
            pltpu.SemaphoreType.DMA((SLOTS,)),
            pltpu.SemaphoreType.DMA((3,)),
            pltpu.SemaphoreType.DMA((3,)),
        ],
        compiler_params=pltpu.CompilerParams(
            collective_id=0, has_side_effects=True, vmem_limit_bytes=35 * 2**20
        ),
        cost_estimate=pl.CostEstimate(
            flops=8 * total * WIDTH * UNITS, bytes_accessed=24 * 2**20, transcendentals=0
        ),
    )(ids, tokens, grad_out, wg, wu, wd)


GRAD_COLUMNS = 640


def grads_kernel(
    mown, gat, tokt, hidt, hh, mixed, grad_gate, grad_up, grad_down,
    mbuf, gbuf, ubuf, dbuf, sems, msem,
):
    total = SLOTS * ROWS
    mbuf[...] = mown[...].astype(BF16)
    mcopy = pltpu.make_async_copy(mbuf, mixed, msem)
    mcopy.start()
    tok_t = tokt[...]
    sc = gat[:, :, WIDTH:].reshape(total, WIDTH)
    blocks = []
    for n in range(UNITS // GRAD_COLUMNS):
        cols = pl.ds(n * GRAD_COLUMNS, GRAD_COLUMNS)
        slot = n % 2
        copies = [
            pltpu.make_async_copy(gbuf.at[slot], grad_gate.at[:, cols], sems.at[0, slot]),
            pltpu.make_async_copy(ubuf.at[slot], grad_up.at[:, cols], sems.at[1, slot]),
            pltpu.make_async_copy(dbuf.at[slot], grad_down.at[cols, :], sems.at[2, slot]),
        ]
        blocks.append(copies)
        for k, buf in enumerate((gbuf, ubuf, dbuf)):
            if n >= 2:
                blocks[n - 2][k].wait()
            if k < 2:
                right = hh[:, k + 1, :, cols].reshape(total, GRAD_COLUMNS)
                buf[slot] = jnp.dot(tok_t, right, preferred_element_type=F32)
            else:
                buf[slot] = jnp.dot(hidt[cols, :], sc, preferred_element_type=F32)
            copies[k].start()
    for copies in blocks[-2:]:
        for copy in copies:
            copy.wait()
    mcopy.wait()


def grads(mown, gat, tokt, hidt, hh):
    total = SLOTS * ROWS
    vmem = pl.BlockSpec(memory_space=pltpu.VMEM)
    hbm = pl.BlockSpec(memory_space=pl.ANY)
    return pl.pallas_call(
        grads_kernel,
        name="grads",
        out_shape=(
            jax.ShapeDtypeStruct((ROWS, WIDTH), BF16),
            jax.ShapeDtypeStruct((WIDTH, UNITS), F32),
            jax.ShapeDtypeStruct((WIDTH, UNITS), F32),
            jax.ShapeDtypeStruct((UNITS, WIDTH), F32),
        ),
        in_specs=[vmem] * 5,
        out_specs=(hbm,) * 4,
        scratch_shapes=[
            pltpu.VMEM((ROWS, WIDTH), BF16),
            pltpu.VMEM((2, WIDTH, GRAD_COLUMNS), F32),
            pltpu.VMEM((2, WIDTH, GRAD_COLUMNS), F32),
            pltpu.VMEM((2, GRAD_COLUMNS, WIDTH), F32),
            pltpu.SemaphoreType.DMA((3, 2)),
            pltpu.SemaphoreType.DMA,
        ],
        compiler_params=pltpu.CompilerParams(vmem_limit_bytes=32 * 2**20),
        cost_estimate=pl.CostEstimate(
            flops=6 * total * WIDTH * UNITS, bytes_accessed=12 * 2**20, transcendentals=0
        ),
    )(mown, gat, tokt, hidt, hh)


def shards(tokens, segment_ids, gate_weight, up_weight, down_weight, grad_out):
    ids = segment_ids.reshape(SLOTS, ROWS)
    outs = exchange(ids, tokens, grad_out, gate_weight, up_weight, down_weight)
    return grads(*outs)


def solution(mesh):
    placed = (
        P("tensor", "dp"),
        P(),
        P("dp", "tensor"),
        P("dp", "tensor"),
        P("tensor", "dp"),
        P("tensor", "dp"),
    )
    return jax.shard_map(
        shards,
        mesh=mesh,
        in_specs=placed,
        out_specs=(P("tensor", "dp"), P("dp", "tensor"), P("dp", "tensor"), P("tensor", "dp")),
        check_vma=False,
    )
```

time: 475 us -> 126 us (0.27)
  waiting for transfers between devices: 372 us -> 0 us
  Pallas kernels: 0 us -> 122 us
  matrix products: 51.8 us -> 0 us
  other arithmetic: 23.5 us -> 0 us
  between operations: 13.8 us -> 0.65 us
  local copies, waits for them, and re-layouts: 13.1 us -> 2.49 us
    psum x1 -> x0, waiting for transfers between devices: 264 us -> none  [shards(): summed = lax.psum(jnp.stack((gate_part, up_part), axis=1), 'dp')]
    pallas_call x0 -> x2, Pallas kernels: none -> 122 us  [the longest x1 113 us: exchange(): pl.pallas_call(exchange_kernel, name='exchange', out_shape=(pltpu.VMEM((R...]
    all_gather x2 -> x0, waiting for transfers between devices: 72.6 us -> none  [the longest x1 48.5 us: shards(): gathered = lax.all_gather(tokens, 'tensor', axis=0, tiled=True)]
    dot_general x7 -> x0, matrix products: 51.8 us -> none  [the longest x3 28.5 us: contract_rows(): lax.dot_general(left, right, (((0,), (0,)), ((), ())), preferred_element_...]
    reduce_scatter x1 -> x0, waiting for transfers between devices: 34.7 us -> none  [shards(): lax.psum_scatter(jnp.dot(block, down_weight, preferred_element_type=jnp.f...]
    another operation x1 -> x0, other arithmetic: 12 us -> none  [shards(): summed = lax.psum(jnp.stack((gate_part, up_part), axis=1), 'dp')]
    unnamed x14 -> x6, local copies, waits for them, and re-layouts: 13 us -> 2.49 us
    convert_element_type x3 -> x0, other arithmetic: 9.95 us -> none  [the longest x1 6.68 us: shards(): hidden = (gate * jax.nn.sigmoid(gate) * up).astype(jnp.bfloat16)]
  transfers between devices with their start and end apart: 4 -> 0, of which waited for: 4 -> 0; matrix products, arithmetic and copies ran while one was open for 14% -> 0% of each run, Pallas kernels for 0% -> 0%
where the time goes in v1:
time: 126 us
  Pallas kernels  122 us (97%)
  local copies, waits for them, and re-layouts  2.49 us (2%)
    pallas_call x1, Pallas kernels, exchange(): pl.pallas_call(exchange_kernel, name='exchange', out_shape=(pltpu.VMEM((R...  113 us
    pallas_call x1, Pallas kernels, grads(): pl.pallas_call(grads_kernel, name='grads', out_shape=(jax.ShapeDtypeStruc...  9.23 us

profile of v1, /device:TPU:8, one launch (start us, length us, event | category | flops | bytes accessed | tf_op | source)
XLA Modules:
  0.0 125.5 jit_solution(7881277377290228794)
XLA Ops:
  0.6 0.0 copy-start
  0.6 0.9 copy-done
  1.5 0.0 copy-start.1
  1.5 0.9 copy-done.1
  2.4 0.0 copy-start.2
  2.4 0.7 copy-done.2
  3.1 113.2 %exchange.1 = (f32[128,512]{1,0:T(8,128)S(1)}, bf16[8,128,1024]{2,1,0:T(8,128)(2,1)S(1)}, bf16[512,1024]{1,0:T(8,128)(2,1)S(1)}, bf16[1920,1024]{1,0:T(8,128)(2,1)S(1)}, bf16[8,3,128,1920]{3,2,1,0:T(8,128)(2,1)S(1)}) custom-call(s32[8,128]{1,0:T(8,128)S(1)} %bitcast.1, bf16[128,512]{1,0:T(8,128)(2,1)S(1)} %copy-done, bf16[128,512]{1,0:T(8,128)(2,1)S(1)} %copy-done.1, ...), custom_call_target="tpu_custom_call" | custom-call | flops 8053063680 | bytes 25165824 | tf_op jit(solution)/shard_map/exchange/pallas_call | solution.py:409
  116.3 9.2 %grads.1 = (bf16[128,512]{1,0:T(8,128)(2,1)}, f32[512,1920]{1,0:T(8,128)}, f32[512,1920]{1,0:T(8,128)}, f32[1920,512]{1,0:T(8,128)}) custom-call(f32[128,512]{1,0:T(8,128)S(1)} %get-tuple-element.9.mown, bf16[8,128,1024]{2,1,0:T(8,128)(2,1)S(1)} %get-tuple-element.10.gat, bf16[512,1024]{1,0:T(8,128)(2,1)S(1)} %get-tuple-element.11.tokt, ...), custom_call_target="tpu_custom_call" | custom-call | flops 6039797760 | bytes 12582912 | tf_op jit(solution)/shard_map/grads/pallas_call | solution.py:504
Async XLA Ops:
  0.6 0.9 copy-start
  1.5 0.9 copy-start.1
  2.4 0.7 copy-start.2
